TPU v7x, 32 devices: a whole 2x2x4 slice. The times are simulated.
32 devices in a mesh: dp: 8 (over y, x, core), mod: 4 (over z).
Axes of the slice: x: 2, y: 2, z: 4, core: 2. Of those that a mesh axis runs over, the one named last changes fastest.
Arguments:
- block_input: bfloat16 [2, 16384, 768], P(None, ('dp', 'mod')), may hold values from -6 to 6
- grad_out: bfloat16 [2, 16384, 768], P(None, ('dp', 'mod')), may hold values from -6 to 6
- long_flag: int32 [2, 32], P(None, ('dp', 'mod')), may hold values from 0 to 1, as said below
- valid_mask: int32 [2, 16384], P(None, ('dp', 'mod')), may hold values from 0 to 1, as said below
- labels: int32 [2, 128], P(None, ('dp', 'mod')), may hold values from 0 to 999
- tsteps: int32 [2, 128], P(None, ('dp', 'mod')), may hold values from 0 to 999
- time_table: bfloat16 [1000, 768], replicated, may hold values from -5 to 5
- class_table: bfloat16 [1000, 768], replicated, may hold values from -5 to 5
- w_ada: bfloat16 [768, 4608], P(None, 'mod'), may hold values from -0.21875 to 0.21875
- b_ada: bfloat16 [4608], P('mod'), may hold values from -3 to 3
- w_qkv: bfloat16 [768, 2304], P('mod'), may hold values from -0.21875 to 0.21875
- qv_bias: bfloat16 [1536], P('mod'), may hold values from -2 to 2
- w_proj: bfloat16 [768, 768], P('mod'), may hold values from -0.875 to 0.875
- proj_bias: bfloat16 [768], P('mod'), may hold values from -2 to 2
- w_fc1: bfloat16 [768, 3072], P('mod'), may hold values from -0.21875 to 0.21875
- fc1_bias: bfloat16 [3072], P('mod'), may hold values from -2 to 2
- w_fc2: bfloat16 [3072, 768], P('mod'), may hold values from -0.109375 to 0.109375
- fc2_bias: bfloat16 [768], P('mod'), may hold values from -2 to 2
- rel_table: bfloat16 [12, 1023], P('mod'), may hold values from -5 to 5
Outputs:
- block_output: bfloat16 [2, 16384, 768], P(None, ('dp', 'mod'))
- grad_input: bfloat16 [2, 16384, 768], P(None, ('dp', 'mod'))
- grad_time_table: float32 [1000, 768], P('mod')
- grad_class_table: float32 [1000, 768], P('mod')
- grad_w_ada: float32 [768, 4608], P(None, 'mod')
- grad_b_ada: float32 [4608], P('mod')
- grad_w_qkv: float32 [768, 2304], P('mod')
- grad_qv_bias: float32 [1536], P('mod')
- grad_w_proj: float32 [768, 768], P('mod')
- grad_proj_bias: float32 [768], P('mod')
- grad_w_fc1: float32 [768, 3072], P('mod')
- grad_fc1_bias: float32 [3072], P('mod')
- grad_w_fc2: float32 [3072, 768], P('mod')
- grad_fc2_bias: float32 [768], P('mod')
- grad_rel_table: float32 [12, 1023], P('mod')
Inputs may be any that keep to these rules, and one draw needn't show every extreme that they name: `long_flag`: 1 marks a buffer holding one sample of 512 tokens; 0 a buffer holding 4 samples of 128 tokens. `valid_mask`: each segment of 128 tokens of a buffer is valid or padding as a whole; the first segment of every buffer is valid, and all of a buffer with long_flag 1 is valid.
All inputs are finite; a program needn't handle non-finite values.
Results may differ from a plain program's by a relative error of at most 0.015.
Values may be sent and summed in bfloat16 or wider, within the bound.
No kernel may reach another device: no remote copies, remote signals or barrier semaphores. Data moves between devices by JAX's collectives and lax.ppermute only.
A program may use at most 256 MiB of HBM per device.

v0:
```python
from functools import partial
import jax
import jax.numpy as jnp
from jax import lax
from jax.sharding import PartitionSpec as P

D = 768
H = 12
HD = 64
FF = 3072
NCLS = 1000
NT = 1000
LLONG = 512
LSHORT = 128
QB = 512
MICRO = 2
SEGS = 4
HIGH = lax.Precision.HIGHEST


def norm_parts(values):
    centred = values - jnp.mean(values, axis=1, keepdims=True)
    inverse_std = lax.rsqrt(jnp.mean(centred * centred, axis=1, keepdims=True) + 1e-06)
    return (centred * inverse_std, inverse_std)


def norm_backward(grad_norm, normed, inverse_std):
    return inverse_std * (
        grad_norm
        - jnp.mean(grad_norm, axis=1, keepdims=True)
        - normed * jnp.mean(grad_norm * normed, axis=1, keepdims=True)
    )


def bias_block(table, start_row, block_rows, length):
    heads = table.shape[0]
    padded = jnp.pad(table, ((0, 0), (0, 1)))
    width = block_rows + length
    tiled = jnp.broadcast_to(padded[:, None, :], (heads, block_rows, width))
    flat = tiled.reshape(heads, block_rows * width)[:, : block_rows * (width - 1)]
    skewed = flat.reshape(heads, block_rows, width - 1)
    return skewed[:, :, block_rows - 1 : block_rows - 1 + length]


def local(
    block_input,
    grad_out,
    long_flag,
    valid_mask,
    labels,
    tsteps,
    time_table,
    class_table,
    w_ada,
    b_ada,
    w_qkv,
    qv_bias,
    w_proj,
    proj_bias,
    w_fc1,
    fc1_bias,
    w_fc2,
    fc2_bias,
    rel_table,
):
    f32 = jnp.float32
    bf16 = jnp.bfloat16
    scale = HD ** (-0.5)
    mod_count = lax.axis_size("mod")
    mod_index = lax.axis_index("mod")
    (
        full_qkv,
        full_qv_bias,
        full_proj,
        full_proj_bias,
        full_fc1,
        full_fc1_bias,
        full_fc2,
        full_fc2_bias,
        full_table,
    ) = (
        lax.all_gather(w_qkv, "mod", axis=0, tiled=True),
        lax.all_gather(qv_bias, "mod", axis=0, tiled=True),
        lax.all_gather(w_proj, "mod", axis=0, tiled=True),
        lax.all_gather(proj_bias, "mod", axis=0, tiled=True),
        lax.all_gather(w_fc1, "mod", axis=0, tiled=True),
        lax.all_gather(fc1_bias, "mod", axis=0, tiled=True),
        lax.all_gather(w_fc2, "mod", axis=0, tiled=True),
        lax.all_gather(fc2_bias, "mod", axis=0, tiled=True),
        lax.all_gather(rel_table, "mod", axis=0, tiled=True),
    )
    qkv_bias = jnp.concatenate(
        [full_qv_bias[:D].astype(f32), jnp.zeros((D,), f32), full_qv_bias[D:].astype(f32)]
    )
    table_float = full_table.astype(f32)
    ada_bias = b_ada.astype(f32)
    ada_weight = w_ada.astype(f32)
    cond = time_table[tsteps].astype(f32) + class_table[labels].astype(f32)
    act_value, silu_pull = jax.vjp(jax.nn.silu, cond)
    act_low = act_value.astype(bf16)
    grad_qkv_w = jnp.zeros(full_qkv.shape, f32)
    grad_qkv_b = jnp.zeros((3 * D,), f32)
    grad_proj_w = jnp.zeros(full_proj.shape, f32)
    grad_proj_b = jnp.zeros((D,), f32)
    grad_fc1_w = jnp.zeros(full_fc1.shape, f32)
    grad_fc1_b = jnp.zeros((FF,), f32)
    grad_fc2_w = jnp.zeros(full_fc2.shape, f32)
    grad_fc2_b = jnp.zeros((D,), f32)
    grad_table = jnp.zeros(full_table.shape, f32)
    grad_ada_w = jnp.zeros(w_ada.shape, f32)
    grad_ada_b = jnp.zeros(b_ada.shape, f32)
    outputs = []
    input_grads = []
    cond_pieces = []
    positions = jnp.arange(LLONG)
    slots = jnp.arange(SEGS)
    for micro_step in range(MICRO):
        group_act = lax.all_gather(act_low[micro_step], "mod", axis=0, tiled=True)
        columns = jnp.dot(group_act, w_ada, preferred_element_type=f32) + ada_bias
        modulation = lax.all_to_all(columns, "mod", split_axis=0, concat_axis=1, tiled=True)
        is_long = long_flag[micro_step, 0]
        owner = jnp.where(is_long > 0, 0, slots)
        select = (owner[:, None] == slots[None, :]).astype(f32)
        mod_tok = jnp.repeat(jnp.dot(select, modulation, precision=HIGH), LSHORT, axis=0)
        shift1, scale1, gate1, shift2, scale2, gate2 = jnp.split(mod_tok, 6, axis=1)
        valid_row = valid_mask[micro_step]
        valid = valid_row.astype(f32)[:, None]
        sample = jnp.where(is_long > 0, 0, positions // LSHORT)
        allowed = (sample[:, None] == sample[None, :]) & (valid_row[None, :] > 0)
        tokens = block_input[micro_step].astype(f32)
        norm1, inverse1 = norm_parts(tokens)
        entry = (norm1 * (1.0 + scale1) + shift1).astype(bf16)
        qkv_low = (jnp.dot(entry, full_qkv, preferred_element_type=f32) + qkv_bias).astype(bf16)
        query = qkv_low[:, :D].reshape(LLONG, H, HD)
        keys_all = qkv_low[:, D : 2 * D].reshape(LLONG, H, HD)
        values_all = qkv_low[:, 2 * D :].reshape(LLONG, H, HD)

        def block_probs(start):
            scores = jnp.einsum("qhd,khd->hqk", query, keys_all, preferred_element_type=f32) * scale
            scores = scores + bias_block(table_float, start, QB, LLONG)
            scores = jnp.where(allowed[None], scores, -1e30)
            top = jnp.max(scores, axis=-1, keepdims=True)
            expo = jnp.exp(scores - top)
            return expo / jnp.sum(expo, axis=-1, keepdims=True)

        block = 0
        probs = block_probs(block * QB)
        attended_parts = jnp.einsum(
            "hqk,khd->qhd", probs.astype(bf16), values_all, preferred_element_type=f32
        )
        attended = attended_parts.reshape(LLONG, D).astype(bf16)
        attn = jnp.dot(attended, full_proj, preferred_element_type=f32) + full_proj_bias.astype(f32)
        hidden = tokens + valid * gate1 * attn
        norm2, inverse2 = norm_parts(hidden)
        m_in = (norm2 * (1.0 + scale2) + shift2).astype(bf16)
        upper = jnp.dot(m_in, full_fc1, preferred_element_type=f32) + full_fc1_bias.astype(f32)
        gelu_value, gelu_pull = jax.vjp(partial(jax.nn.gelu, approximate=True), upper)
        gelu_low = gelu_value.astype(bf16)
        mlp = jnp.dot(gelu_low, full_fc2, preferred_element_type=f32) + full_fc2_bias.astype(f32)
        outputs.append((hidden + valid * gate2 * mlp).astype(bf16))
        grad_y = grad_out[micro_step].astype(f32)
        grad_mlp = (grad_y * valid * gate2).astype(bf16)
        grad_gate2 = grad_y * valid * mlp
        grad_fc2_w = grad_fc2_w + jnp.dot(gelu_low.T, grad_mlp, preferred_element_type=f32)
        grad_fc2_b = grad_fc2_b + jnp.sum(grad_mlp.astype(f32), axis=0)
        grad_gelu = jnp.einsum("td,fd->tf", grad_mlp, full_fc2, preferred_element_type=f32)
        grad_upper = gelu_pull(grad_gelu)[0].astype(bf16)
        grad_fc1_w = grad_fc1_w + jnp.dot(m_in.T, grad_upper, preferred_element_type=f32)
        grad_fc1_b = grad_fc1_b + jnp.sum(grad_upper.astype(f32), axis=0)
        grad_min = jnp.einsum("tf,df->td", grad_upper, full_fc1, preferred_element_type=f32)
        grad_scale2 = grad_min * norm2
        grad_hidden = grad_y + norm_backward(grad_min * (1.0 + scale2), norm2, inverse2)
        grad_attn = (grad_hidden * valid * gate1).astype(bf16)
        grad_gate1 = grad_hidden * valid * attn
        grad_proj_w = grad_proj_w + jnp.dot(attended.T, grad_attn, preferred_element_type=f32)
        grad_proj_b = grad_proj_b + jnp.sum(grad_attn.astype(f32), axis=0)
        grad_attended = (
            jnp.einsum("te,de->td", grad_attn, full_proj, preferred_element_type=f32)
            .astype(bf16)
            .reshape(LLONG, H, HD)
        )
        block = 0
        start = block * QB
        probs = block_probs(start)
        grad_probs = jnp.einsum(
            "qhd,khd->hqk", grad_attended, values_all, preferred_element_type=f32
        )
        delta = jnp.sum(grad_probs * probs, axis=-1, keepdims=True)
        grad_scores = (probs * (grad_probs - delta)).astype(bf16)
        grad_query_parts = (
            jnp.einsum("hqk,khd->qhd", grad_scores, keys_all, preferred_element_type=f32) * scale
        )
        grad_keys = (
            jnp.einsum("hqk,qhd->khd", grad_scores, query, preferred_element_type=f32) * scale
        )
        grad_values = jnp.einsum(
            "hqk,qhd->khd", probs.astype(bf16), grad_attended, preferred_element_type=f32
        )
        bias_value, bias_pull = jax.vjp(
            partial(bias_block, start_row=start, block_rows=QB, length=LLONG), table_float
        )
        grad_table = grad_table + bias_pull(grad_scores.astype(f32))[0]
        grad_qkv = jnp.concatenate(
            [
                grad_query_parts.reshape(LLONG, D),
                grad_keys.reshape(LLONG, D),
                grad_values.reshape(LLONG, D),
            ],
            axis=1,
        ).astype(bf16)
        grad_qkv_w = grad_qkv_w + jnp.dot(entry.T, grad_qkv, preferred_element_type=f32)
        grad_qkv_b = grad_qkv_b + jnp.sum(grad_qkv.astype(f32), axis=0)
        grad_entry = jnp.einsum("te,de->td", grad_qkv, full_qkv, preferred_element_type=f32)
        grad_scale1 = grad_entry * norm1
        input_grads.append(
            (grad_hidden + norm_backward(grad_entry * (1.0 + scale1), norm1, inverse1)).astype(bf16)
        )
        grad_mod_tok = jnp.concatenate(
            [grad_entry, grad_scale1, grad_gate1, grad_min, grad_scale2, grad_gate2], axis=1
        )
        grad_mod_seg = jnp.sum(grad_mod_tok.reshape(SEGS, LSHORT, 6 * D), axis=1)
        grad_modulation = jnp.dot(select.T, grad_mod_seg, precision=HIGH)
        grad_columns = lax.all_to_all(
            grad_modulation.astype(jnp.bfloat16), "mod", split_axis=1, concat_axis=0, tiled=True
        ).astype(grad_modulation.dtype)
        grad_ada_w = grad_ada_w + jnp.dot(group_act.astype(f32).T, grad_columns, precision=HIGH)
        grad_ada_b = grad_ada_b + jnp.sum(grad_columns, axis=0)
        cond_share = jnp.dot(grad_columns, ada_weight.T, precision=HIGH)
        cond_pieces.append(
            lax.psum_scatter(
                cond_share.astype(jnp.bfloat16), "mod", scatter_dimension=0, tiled=True
            ).astype(jnp.float32)
        )
    grad_act = jnp.stack(cond_pieces, axis=0)
    grad_cond = silu_pull(grad_act)[0].reshape(MICRO * SEGS, D)
    time_onehot = (tsteps.reshape(MICRO * SEGS)[:, None] == jnp.arange(NT)[None, :]).astype(f32)
    class_onehot = (labels.reshape(MICRO * SEGS)[:, None] == jnp.arange(NCLS)[None, :]).astype(f32)
    grad_time = jnp.dot(time_onehot.T, grad_cond, precision=HIGH)
    grad_class = jnp.dot(class_onehot.T, grad_cond, precision=HIGH)
    grad_qv = jnp.concatenate([grad_qkv_b[:D], grad_qkv_b[2 * D :]])
    summed = lax.psum(
        (
            grad_time,
            grad_class,
            grad_qkv_w,
            grad_qv,
            grad_proj_w,
            grad_proj_b,
            grad_fc1_w,
            grad_fc1_b,
            grad_fc2_w,
            grad_fc2_b,
            grad_table,
        ),
        ("dp", "mod"),
    )
    shares = tuple(
        (
            lax.dynamic_slice_in_dim(
                whole, mod_index * (whole.shape[0] // mod_count), whole.shape[0] // mod_count, 0
            )
            for whole in summed
        )
    )
    ada_w_total, ada_b_total = (
        lax.psum(grad_ada_w.astype(jnp.bfloat16), "dp").astype(jnp.float32),
        lax.psum(grad_ada_b.astype(jnp.bfloat16), "dp").astype(jnp.float32),
    )
    return (
        jnp.stack(outputs, axis=0),
        jnp.stack(input_grads, axis=0),
        shares[0],
        shares[1],
        ada_w_total,
        ada_b_total,
        shares[2],
        shares[3],
        shares[4],
        shares[5],
        shares[6],
        shares[7],
        shares[8],
        shares[9],
        shares[10],
    )


def solution(mesh):
    in_specs = (
        P(None, ("dp", "mod"), None),
        P(None, ("dp", "mod"), None),
        P(None, ("dp", "mod")),
        P(None, ("dp", "mod")),
        P(None, ("dp", "mod")),
        P(None, ("dp", "mod")),
        P(),
        P(),
        P(None, "mod"),
        P("mod"),
        P("mod", None),
        P("mod"),
        P("mod", None),
        P("mod"),
        P("mod", None),
        P("mod"),
        P("mod", None),
        P("mod"),
        P("mod", None),
    )
    out_specs = (
        P(None, ("dp", "mod"), None),
        P(None, ("dp", "mod"), None),
        P("mod", None),
        P("mod", None),
        P(None, "mod"),
        P("mod"),
        P("mod", None),
        P("mod"),
        P("mod", None),
        P("mod"),
        P("mod", None),
        P("mod"),
        P("mod", None),
        P("mod"),
        P("mod", None),
    )
    return jax.shard_map(local, mesh=mesh, in_specs=in_specs, out_specs=out_specs, check_vma=False)
```

profile of v0, /device:TPU:0, one launch (start us, length us, event | category | flops | bytes accessed | tf_op | source)
XLA Modules:
  0.0 1603.2 jit_solution(13607103833708870394)
XLA Ops:
  16.0 15.2 all-gather.1
  42.9 12.5 all-reduce.12
  56.3 12.0 all-gather.2
  68.3 13.3 all-gather.3
  81.7 11.8 broadcast_in_dim.58
  93.5 11.0 pad.64
  104.5 39.7 %copy.161 = f32[2,8,512,1024]{3,1,2,0:T(8,128)} copy(f32[2,8,512,1024]{3,2,1,0:T(8,128)S(1)} %bitcast.259) | data formatting | bytes 67108864
  144.2 22.8 %slice.108 = f32[12,523776]{1,0:T(8,128)} slice(f32[12,524288]{1,0:T(8,128)} %bitcast.262), slice={[0:12], [0:523776]} | slice | bytes 50282496 | tf_op jit(solution)/shard_map/slice | solution.py:40
  166.9 54.2 %reshape.401 = f32[12,512,1023]{2,1,0:T(8,128)} reshape(f32[12,523776]{1,0:T(8,128)} %slice.108) | data formatting | bytes 50282496 | tf_op jit(solution)/shard_map/reshape | solution.py:41
  221.2 13.4 slice.109
  234.6 12.8 copy.158
  248.6 13.2 all-gather.4
  262.5 14.6 all-gather
  315.1 11.9 add_select_fusion
  327.0 15.2 fusion.146
  342.2 12.3 fusion.77
  399.2 11.5 fusion.80
  454.4 11.7 add_select_fusion.1
  466.1 15.2 fusion.147
  481.3 12.4 fusion.71
  535.7 12.3 fusion.74
  548.0 12.0 multiply_reduce_fusion.1
  672.1 35.2 %reshape.419 = bf16[12,523776]{1,0:T(8,128)(2,1)} reshape(bf16[12,512,1023]{2,1,0:T(8,128)(2,1)} %pad.40.clone) | data formatting | bytes 25141248 | tf_op jit(solution)/shard_map/transpose(jvp())/reshape | solution.py:41
  715.9 35.8 %copy.163 = f32[2,8,512,1024]{3,2,1,0:T(8,128)} copy(f32[2,8,512,1024]{3,1,2,0:T(8,128)S(1)} %bitcast.260) | data formatting | bytes 67108864
  760.7 10.7 pad.37.clone
  771.5 34.8 %reshape.416 = bf16[12,523776]{1,0:T(8,128)(2,1)} reshape(bf16[12,512,1023]{2,1,0:T(8,128)(2,1)} %pad.37.clone) | data formatting | bytes 25141248 | tf_op jit(solution)/shard_map/transpose(jvp())/reshape | solution.py:41
  814.8 35.9 %copy.162 = f32[2,8,512,1024]{3,2,1,0:T(8,128)} copy(f32[2,8,512,1024]{3,1,2,0:T(8,128)S(1)} %bitcast.261) | data formatting | bytes 67108864
  876.7 16.9 %all-reduce.11 = (bf16[16,768]{1,0:T(8,128)(2,1)S(1)}, bf16[16,768]{1,0:T(8,128)(2,1)S(1)}) all-reduce(bf16[16,768]{1,0:T(8,128)(2,1)S(1)} %convolution_convert_fusion.4, bf16[16,768]{1,0:T(8,128)(2,1)S(1)} %convolution_convert_fusion.5), channel_id=5, replica_groups=mesh['dp'=8,'mod'=4] {'mod'}, use_global_device_ids=true, to_apply=%region_25.26.clone | all-reduce | flops 24576 | bytes 98304
  905.0 82.4 %all-reduce.19.cloned.1.call-done = (f32[1536]{0:T(1024)}, f32[768]{0:T(1024)}, f32[3072]{0:T(1024)}, f32[768]{0:T(1024)}, f32[12,1023]{1,0:T(8,128)}) async-done(((f32[1536]{0:T(1024)}, f32[768]{0:T(1024)}, f32[3072]{0:T(1024)}, f32[768]{0:T(1024)}, f32[12,1023]{1,0:T(8,128)}), (f32[1536]{0:T(1024)}, f32[768]{0:T(1024)}, f32[3072]{0:T(1024)}, f32[768]{0:T(1024)}, ...) | async-done | bytes 73696 | tf_op jit(solution)/shard_map/psum | solution.py:241
  994.2 12.3 psum.94
  1007.2 44.8 %all-reduce.17.cloned.1.call-done = bf16[768,1152]{1,0:T(8,128)(2,1)} async-done(((bf16[768,1152]{1,0:T(8,128)(2,1)}), bf16[768,1152]{1,0:T(8,128)(2,1)}) %all-reduce.17.cloned.1.call-update) | async-done | bytes 1769488 | tf_op jit(solution)/shard_map/psum | solution.py:266
  1055.4 525.1 %all-reduce.21.cloned.1.call-done = (f32[1000,768]{1,0:T(8,128)}, f32[1000,768]{1,0:T(8,128)}, f32[768,2304]{1,0:T(8,128)}, f32[768,768]{1,0:T(8,128)}, f32[768,3072]{1,0:T(8,128)}, /*index=5*/f32[3072,768]{1,0:T(8,128)}) async-done(((f32[1000,768]{1,0:T(8,128)}, f32[1000,768]{1,0:T(8,128)}, f32[768,2304]{1,0:T(8,128)}, f32[768,768]{1,0:T(8,128)}, f32[768,3072]{1,0:T(8,128)}, ...) | async-done | bytes 34455568 | tf_op jit(solution)/shard_map/psum | solution.py:241
  (497 shorter events, 389.6 us)
Async XLA Ops:
  7.2 24.6 %copy-start = (bf16[768,1152]{1,0:T(8,128)(2,1)S(1)}, bf16[768,1152]{1,0:T(8,128)(2,1)}, u32[]{:S(2)}) copy-start(bf16[768,1152]{1,0:T(8,128)(2,1)} %param.27) | copy-start | bytes 5308420
  7.2 34.0 %copy-start.107 = (u32[32]{0:T(128)S(1)}, u32[32]{0:T(128)}, u32[]{:S(2)}) copy-start(u32[32]{0:T(128)} %constant.123) | copy-start | bytes 388
  7.2 31.6 %copy-start.112 = (s32[2,4]{1,0:T(2,128)S(1)}, s32[2,4]{1,0:T(2,128)}, u32[]{:S(2)}) copy-start(s32[2,4]{1,0:T(2,128)} %param.23) | copy-start | bytes 100
  7.2 30.9 %copy-start.111 = (s32[2,4]{1,0:T(2,128)S(1)}, s32[2,4]{1,0:T(2,128)}, u32[]{:S(2)}) copy-start(s32[2,4]{1,0:T(2,128)} %param.24) | copy-start | bytes 100
  7.2 32.2 %copy-start.109 = (s32[2,1]{0,1:T(1,128)S(1)}, s32[2,1]{0,1:T(1,128)}, u32[]{:S(2)}) copy-start(s32[2,1]{0,1:T(1,128)} %param.21) | copy-start | bytes 28
  7.2 35.2 %copy-start.116 = (bf16[192]{0:T(256)(128)(2,1)S(1)}, bf16[192]{0:T(256)(128)(2,1)}, u32[]{:S(2)}) copy-start(bf16[192]{0:T(256)(128)(2,1)} %param.32) | copy-start | bytes 1156
  7.3 35.4 %copy-start.117 = (bf16[192]{0:T(256)(128)(2,1)S(1)}, bf16[192]{0:T(256)(128)(2,1)}, u32[]{:S(2)}) copy-start(bf16[192]{0:T(256)(128)(2,1)} %param.36) | copy-start | bytes 1156
  7.3 48.1 %copy-start.8 = (bf16[2,512,768]{2,1,0:T(8,128)(2,1)S(1)}, bf16[2,512,768]{2,1,0:T(8,128)(2,1)}, u32[]{:S(2)}) copy-start(bf16[2,512,768]{2,1,0:T(8,128)(2,1)} %param.19) | copy-start | bytes 4718596
  7.3 295.3 %all-gather.10.cloned.1.call-start = ((), (), s32[]{:S(2)}) async-start(), calls=%async_computation.4 | async-start | bytes 4423680 | tf_op jit(solution)/shard_map/all_gather | solution.py:82
  8.0 346.5 %all-gather.12.cloned.1.call-start = ((), (), s32[]{:S(2)}) async-start(), calls=%async_computation.5 | async-start | bytes 1474560 | tf_op jit(solution)/shard_map/all_gather | solution.py:84
  8.8 47.5 %copy-start.110 = (bf16[384]{0:T(512)(128)(2,1)S(1)}, bf16[384]{0:T(512)(128)(2,1)}, u32[]{:S(2)}) copy-start(bf16[384]{0:T(512)(128)(2,1)} %param.30) | copy-start | bytes 2308
  8.8 59.5 %copy-start.102 = (bf16[3,1023]{1,0:T(4,128)(2,1)S(1)}, bf16[3,1023]{1,0:T(4,128)(2,1)}, u32[]{:S(2)}) copy-start(bf16[3,1023]{1,0:T(4,128)(2,1)} %param.37) | copy-start | bytes 18418
  8.8 356.1 %all-gather.14.cloned.1.call-start = ((), (), s32[]{:S(2)}) async-start(), calls=%async_computation.6 | async-start | bytes 5898240 | tf_op jit(solution)/shard_map/all_gather | solution.py:86
  32.8 251.4 %all-to-all-start.1 = ((f32[4,4,1152]{2,1,0:T(4,128)}), f32[4,4,1152]{2,1,0:T(4,128)S(1)}, u32[]{:S(2)}, u32[]{:S(2)}) async-start(f32[4,4,1152]{2,1,0:T(4,128)} %all_to_all.60), calls=%async_computation.1 | async-start | bytes 147456 | tf_op jit(solution)/shard_map/all_to_all | solution.py:120
  37.5 335.2 %all-gather.16.cloned.1.call-start = ((), (), s32[]{:S(2)}) async-start(), calls=%async_computation.7 | async-start | bytes 5898240 | tf_op jit(solution)/shard_map/all_gather | solution.py:88
  234.6 45.4 %copy-start.101 = (f32[512]{0:T(512)S(1)}, f32[512]{0:T(512)}, u32[]{:S(2)}) copy-start(f32[512]{0:T(512)} %get-tuple-element.24) | copy-start | bytes 6148
  262.5 20.8 %copy-start.106 = (pred[512]{0:T(512)(128)(4,1)S(1)}, pred[512]{0:T(512)(128)(4,1)}, u32[]{:S(2)}) copy-start(pred[512]{0:T(512)(128)(4,1)} %get-tuple-element.28) | copy-start | bytes 1540
  281.6 111.5 %copy-start.87 = (f32[1,512]{1,0:T(1,128)}, f32[1,512]{1,0:T(1,128)S(1)}, u32[]{:S(2)}) copy-start(f32[1,512]{1,0:T(1,128)S(1)} %get-tuple-element.89) | copy-start | bytes 6148
  284.2 11.1 all-to-all-start
  360.5 32.6 %copy-start.84 = (f32[512]{0:T(512)}, f32[512]{0:T(512)S(1)}, u32[]{:S(2)}) copy-start(f32[512]{0:T(512)S(1)} %broadcast_multiply_fusion.8) | copy-start | bytes 6148
  361.7 31.5 %copy-start.89 = (f32[512]{0:T(512)}, f32[512]{0:T(512)S(1)}, u32[]{:S(2)}) copy-start(f32[512]{0:T(512)S(1)} %add_rsqrt_fusion) | copy-start | bytes 6148
  364.8 17.9 %slice-start.3 = ((s8[9437184]{0:T(1024)(128)(4,1)}), s8[1048576]{0:T(1024)(128)(4,1)S(1)}, s32[]{:S(2)}) async-start(s8[9437184]{0:T(1024)(128)(4,1)} %bitcast.279), calls=%async_computation.14 | async-start | bytes 2097152
  410.7 23.8 %copy-start.51 = (bf16[12,64,512]{2,1,0:T(8,128)(2,1)}, bf16[12,64,512]{2,1,0:T(8,128)(2,1)S(1)}, u32[]{:S(2)}) copy-start(bf16[12,64,512]{2,1,0:T(8,128)(2,1)S(1)} %fusion.80) | copy-start | bytes 2359300
  569.5 20.7 %copy-start.68 = (bf16[12,64,512]{2,1,0:T(8,128)(2,1)}, bf16[12,64,512]{2,1,0:T(8,128)(2,1)S(1)}, u32[]{:S(2)}) copy-start(bf16[12,64,512]{2,1,0:T(8,128)(2,1)S(1)} %multiply_convert_fusion.7) | copy-start | bytes 2359300
  571.2 19.1 %copy-start.40 = (bf16[12,64,512]{2,1,0:T(8,128)(2,1)}, bf16[12,64,512]{2,1,0:T(8,128)(2,1)S(1)}, u32[]{:S(2)}) copy-start(bf16[12,64,512]{2,1,0:T(8,128)(2,1)S(1)} %multiply_convert_fusion.8) | copy-start | bytes 2359300
  630.0 232.8 %all-to-all-start.3 = ((bf16[4,4,1152]{2,0,1:T(4,128)(2,1)}), bf16[4,4,1152]{2,0,1:T(4,128)(2,1)S(1)}, u32[]{:S(2)}, u32[]{:S(2)}) async-start(bf16[4,4,1152]{2,0,1:T(4,128)(2,1)} %bitcast.52), calls=%async_computation.3 | async-start | bytes 73728 | tf_op jit(solution)/shard_map/all_to_all | solution.py:223
  633.3 354.1 %all-reduce.19.cloned.1.call-start = ((), (), s32[]{:S(2)}) async-start(), calls=%async_computation.9 | async-start | bytes 188416 | tf_op jit(solution)/shard_map/psum | solution.py:241
  850.7 22.9 %copy-start.79 = (bf16[1,16,768]{2,0,1:T(2,128)(2,1)S(1)}, bf16[1,16,768]{2,0,1:T(2,128)(2,1)}, u32[]{:S(2)}) copy-start(bf16[1,16,768]{2,0,1:T(2,128)(2,1)} %copy-done.78) | copy-start | bytes 73732
  862.9 10.7 all-to-all-start.2
  867.9 184.1 %all-reduce.17.cloned.1.call-start = ((), (), s32[]{:S(2)}) async-start(), calls=%async_computation.8 | async-start | bytes 3538944 | tf_op jit(solution)/shard_map/psum | solution.py:266
  876.1 20.9 %copy-start.113 = (s32[8]{0:T(128)S(1)}, s32[8]{0:T(128)}, u32[]{:S(2)}) copy-start(s32[8]{0:T(128)} %eq.106) | copy-start | bytes 100
  893.7 686.9 %all-reduce.21.cloned.1.call-start = ((), (), s32[]{:S(2)}) async-start(), calls=%async_computation.10 | async-start | bytes 68911104 | tf_op jit(solution)/shard_map/psum | solution.py:241
  (123 other events, 821.8 us)
Sparse Core Ops, SparseCore 0:
  9.7 75.3 all-gather.9
  86.7 29.2 all-gather.11
  117.5 88.5 all-gather.13
  207.5 90.2 all-gather.15
  863.0 124.3 all-reduce.18
  991.1 60.8 all-reduce.16
  1060.1 520.4 all-reduce.20
where the time goes:
time: 1610 us; the launch traced here: 1600 us
  waiting for transfers between devices  666 us (41%)
  local copies, waits for them, and re-layouts  422 us (26%)
  matrix products  242 us (15%)
  other arithmetic  127 us (8%)
  blocking collectives  110 us (7%)
  between operations  18.9 us (1%)
  starting transfers between devices  17.2 us (1%)
    psum x2, waiting for transfers between devices, local(): lax.psum((grad_time, grad_class, grad_qkv_w, grad_qv, grad_proj_w, grad_p...  607 us
    unnamed x305, local copies, waits for them, and re-layouts  182 us
    reshape x3, local copies, waits for them, and re-layouts, bias_block(): skewed = flat.reshape(heads, block_rows, width - 1)  124 us
    psum x1, waiting for transfers between devices, local(): lax.psum(grad_ada_w.astype(jnp.bfloat16), 'dp').astype(jnp.float32)  44.8 us
  transfers between devices with their start and end apart: 11, of which 5 were waited for; matrix products, arithmetic and copies ran while one was open for 32% of the time, Pallas kernels for 0%

commit v1 on v0

--- a/solution.py
+++ b/solution.py
@@ -238,22 +238,21 @@
     grad_time = jnp.dot(time_onehot.T, grad_cond, precision=HIGH)
     grad_class = jnp.dot(class_onehot.T, grad_cond, precision=HIGH)
     grad_qv = jnp.concatenate([grad_qkv_b[:D], grad_qkv_b[2 * D :]])
-    summed = lax.psum(
-        (
-            grad_time,
-            grad_class,
-            grad_qkv_w,
-            grad_qv,
-            grad_proj_w,
-            grad_proj_b,
-            grad_fc1_w,
-            grad_fc1_b,
-            grad_fc2_w,
-            grad_fc2_b,
-            grad_table,
-        ),
-        ("dp", "mod"),
-    )
+    summed = (
+        grad_time,
+        grad_class,
+        grad_qkv_w,
+        grad_qv,
+        grad_proj_w,
+        grad_proj_b,
+        grad_fc1_w,
+        grad_fc1_b,
+        grad_fc2_w,
+        grad_fc2_b,
+        grad_table,
+    )
+    for axis in ("mod", "dp"):
+        summed = lax.psum(summed, axis)
     shares = tuple(
         (
             lax.dynamic_slice_in_dim(

time: 1610 us -> 2620 us (1.63)
  waiting for transfers between devices: 666 us -> 1660 us
    psum x2 -> x4, waiting for transfers between devices: 607 us -> 1590 us  [local(): summed = lax.psum(summed, axis)]
  transfers between devices with their start and end apart: 11 -> 13, of which waited for: 5 -> 6; matrix products, arithmetic and copies ran while one was open for 32% -> 20% of each run, Pallas kernels for 0% -> 0%
where the time goes in v1:
time: 2620 us; the launch traced here: 2610 us
  waiting for transfers between devices  1660 us (63%)
  local copies, waits for them, and re-layouts  423 us (16%)
  matrix products  246 us (9%)
  other arithmetic  127 us (5%)
  blocking collectives  112 us (4%)
    psum x4, waiting for transfers between devices, local(): summed = lax.psum(summed, axis)  1590 us
    unnamed x305, local copies, waits for them, and re-layouts  183 us
    reshape x3, local copies, waits for them, and re-layouts, bias_block(): skewed = flat.reshape(heads, block_rows, width - 1)  124 us
    psum x1, waiting for transfers between devices, local(): lax.psum(grad_ada_w.astype(jnp.bfloat16), 'dp').astype(jnp.float32)  57.5 us
  transfers between devices with their start and end apart: 13, of which 6 were waited for; matrix products, arithmetic and copies ran while one was open for 20% of the time, Pallas kernels for 0%

profile of v1, /device:TPU:0, one launch (start us, length us, event | category | flops | bytes accessed | tf_op | source)
XLA Modules:
  0.0 2606.1 jit_solution(14699535161216014240)
XLA Ops:
  16.0 15.2 all-gather.1
  42.9 12.5 all-reduce.14
  56.3 12.0 all-gather.2
  68.3 13.3 all-gather.3
  81.7 11.8 broadcast_in_dim.58
  93.5 11.0 pad.64
  104.5 39.7 %copy.161 = f32[2,8,512,1024]{3,1,2,0:T(8,128)} copy(f32[2,8,512,1024]{3,2,1,0:T(8,128)S(1)} %bitcast.259) | data formatting | bytes 67108864
  144.2 22.7 slice.108
  166.9 54.3 %reshape.401 = f32[12,512,1023]{2,1,0:T(8,128)} reshape(f32[12,523776]{1,0:T(8,128)} %slice.108) | data formatting | bytes 50282496 | tf_op jit(solution)/shard_map/reshape | solution.py:41
  221.2 13.4 slice.109
  234.6 12.8 copy.158
  248.7 13.2 all-gather.4
  262.5 14.6 all-gather
  315.1 11.9 add_select_fusion
  326.9 15.2 fusion.146
  342.1 12.3 fusion.77
  399.0 11.5 fusion.80
  454.1 11.7 add_select_fusion.1
  465.8 15.2 fusion.147
  480.9 12.3 fusion.71
  535.3 12.3 fusion.74
  547.7 12.0 multiply_reduce_fusion.1
  671.9 35.2 %reshape.419 = bf16[12,523776]{1,0:T(8,128)(2,1)} reshape(bf16[12,512,1023]{2,1,0:T(8,128)(2,1)} %pad.40.clone) | data formatting | bytes 25141248 | tf_op jit(solution)/shard_map/transpose(jvp())/reshape | solution.py:41
  715.6 35.8 %copy.163 = f32[2,8,512,1024]{3,2,1,0:T(8,128)} copy(f32[2,8,512,1024]{3,1,2,0:T(8,128)S(1)} %bitcast.260) | data formatting | bytes 67108864
  771.2 34.8 %reshape.416 = bf16[12,523776]{1,0:T(8,128)(2,1)} reshape(bf16[12,512,1023]{2,1,0:T(8,128)(2,1)} %pad.37.clone) | data formatting | bytes 25141248 | tf_op jit(solution)/shard_map/transpose(jvp())/reshape | solution.py:41
  814.6 35.9 %copy.162 = f32[2,8,512,1024]{3,2,1,0:T(8,128)} copy(f32[2,8,512,1024]{3,1,2,0:T(8,128)S(1)} %bitcast.261) | data formatting | bytes 67108864
  874.0 17.4 all-reduce.13
  905.2 1140.1 %all-reduce.29.cloned.1.call-done = (f32[1000,768]{1,0:T(8,128)}, f32[1000,768]{1,0:T(8,128)}, f32[768,2304]{1,0:T(8,128)}, f32[768,768]{1,0:T(8,128)}, f32[768,3072]{1,0:T(8,128)}, /*index=5*/f32[3072,768]{1,0:T(8,128)}) async-done(((f32[1000,768]{1,0:T(8,128)}, f32[1000,768]{1,0:T(8,128)}, f32[768,2304]{1,0:T(8,128)}, f32[768,768]{1,0:T(8,128)}, f32[768,3072]{1,0:T(8,128)}, ...) | async-done | bytes 34455568 | tf_op jit(solution)/shard_map/psum | solution.py:255
  2050.2 13.7 psum.173
  2064.5 36.6 %all-reduce.23.cloned.1.call-done = (f32[1536]{0:T(1024)}, f32[768]{0:T(1024)}, f32[3072]{0:T(1024)}, f32[768]{0:T(1024)}, f32[12,1023]{1,0:T(8,128)}) async-done(((f32[1536]{0:T(1024)}, f32[768]{0:T(1024)}, f32[3072]{0:T(1024)}, f32[768]{0:T(1024)}, f32[12,1023]{1,0:T(8,128)}), (f32[1536]{0:T(1024)}, f32[768]{0:T(1024)}, f32[3072]{0:T(1024)}, f32[768]{0:T(1024)}, ...) | async-done | bytes 73696 | tf_op jit(solution)/shard_map/psum | solution.py:255
  2107.9 57.5 %all-reduce.21.cloned.1.call-done = bf16[768,1152]{1,0:T(8,128)(2,1)} async-done(((bf16[768,1152]{1,0:T(8,128)(2,1)}), bf16[768,1152]{1,0:T(8,128)(2,1)}) %all-reduce.21.cloned.1.call-update) | async-done | bytes 1769488 | tf_op jit(solution)/shard_map/psum | solution.py:265
  2169.0 414.8 %all-reduce.25.cloned.1.call-done = (f32[1000,768]{1,0:T(8,128)}, f32[1000,768]{1,0:T(8,128)}, f32[768,2304]{1,0:T(8,128)}, f32[768,768]{1,0:T(8,128)}, f32[768,3072]{1,0:T(8,128)}, /*index=5*/f32[3072,768]{1,0:T(8,128)}) async-done(((f32[1000,768]{1,0:T(8,128)}, f32[1000,768]{1,0:T(8,128)}, f32[768,2304]{1,0:T(8,128)}, f32[768,768]{1,0:T(8,128)}, f32[768,3072]{1,0:T(8,128)}, ...) | async-done | bytes 34455568 | tf_op jit(solution)/shard_map/psum | solution.py:255
  (503 shorter events, 404.7 us)
Async XLA Ops:
  7.2 24.6 copy-start
  7.2 34.0 %copy-start.107 = (u32[32]{0:T(128)S(1)}, u32[32]{0:T(128)}, u32[]{:S(2)}) copy-start(u32[32]{0:T(128)} %constant.123) | copy-start | bytes 388
  7.2 31.6 %copy-start.112 = (s32[2,4]{1,0:T(2,128)S(1)}, s32[2,4]{1,0:T(2,128)}, u32[]{:S(2)}) copy-start(s32[2,4]{1,0:T(2,128)} %param.23) | copy-start | bytes 100
  7.2 30.9 %copy-start.111 = (s32[2,4]{1,0:T(2,128)S(1)}, s32[2,4]{1,0:T(2,128)}, u32[]{:S(2)}) copy-start(s32[2,4]{1,0:T(2,128)} %param.24) | copy-start | bytes 100
  7.2 32.2 %copy-start.109 = (s32[2,1]{0,1:T(1,128)S(1)}, s32[2,1]{0,1:T(1,128)}, u32[]{:S(2)}) copy-start(s32[2,1]{0,1:T(1,128)} %param.21) | copy-start | bytes 28
  7.2 35.2 %copy-start.116 = (bf16[192]{0:T(256)(128)(2,1)S(1)}, bf16[192]{0:T(256)(128)(2,1)}, u32[]{:S(2)}) copy-start(bf16[192]{0:T(256)(128)(2,1)} %param.32) | copy-start | bytes 1156
  7.3 35.4 %copy-start.117 = (bf16[192]{0:T(256)(128)(2,1)S(1)}, bf16[192]{0:T(256)(128)(2,1)}, u32[]{:S(2)}) copy-start(bf16[192]{0:T(256)(128)(2,1)} %param.36) | copy-start | bytes 1156
  7.3 48.1 %copy-start.8 = (bf16[2,512,768]{2,1,0:T(8,128)(2,1)S(1)}, bf16[2,512,768]{2,1,0:T(8,128)(2,1)}, u32[]{:S(2)}) copy-start(bf16[2,512,768]{2,1,0:T(8,128)(2,1)} %param.19) | copy-start | bytes 4718596
  7.3 295.2 %all-gather.10.cloned.1.call-start = ((), (), s32[]{:S(2)}) async-start(), calls=%async_computation.4 | async-start | bytes 4423680 | tf_op jit(solution)/shard_map/all_gather | solution.py:82
  8.0 346.4 %all-gather.12.cloned.1.call-start = ((), (), s32[]{:S(2)}) async-start(), calls=%async_computation.5 | async-start | bytes 1474560 | tf_op jit(solution)/shard_map/all_gather | solution.py:84
  8.8 47.5 %copy-start.110 = (bf16[384]{0:T(512)(128)(2,1)S(1)}, bf16[384]{0:T(512)(128)(2,1)}, u32[]{:S(2)}) copy-start(bf16[384]{0:T(512)(128)(2,1)} %param.30) | copy-start | bytes 2308
  8.8 59.5 %copy-start.102 = (bf16[3,1023]{1,0:T(4,128)(2,1)S(1)}, bf16[3,1023]{1,0:T(4,128)(2,1)}, u32[]{:S(2)}) copy-start(bf16[3,1023]{1,0:T(4,128)(2,1)} %param.37) | copy-start | bytes 18418
  8.8 355.9 %all-gather.14.cloned.1.call-start = ((), (), s32[]{:S(2)}) async-start(), calls=%async_computation.6 | async-start | bytes 5898240 | tf_op jit(solution)/shard_map/all_gather | solution.py:86
  32.8 251.4 %all-to-all-start.1 = ((f32[4,4,1152]{2,1,0:T(4,128)}), f32[4,4,1152]{2,1,0:T(4,128)S(1)}, u32[]{:S(2)}, u32[]{:S(2)}) async-start(f32[4,4,1152]{2,1,0:T(4,128)} %all_to_all.60), calls=%async_computation.1 | async-start | bytes 147456 | tf_op jit(solution)/shard_map/all_to_all | solution.py:120
  37.5 335.1 %all-gather.16.cloned.1.call-start = ((), (), s32[]{:S(2)}) async-start(), calls=%async_computation.7 | async-start | bytes 5898240 | tf_op jit(solution)/shard_map/all_gather | solution.py:88
  234.6 45.4 %copy-start.101 = (f32[512]{0:T(512)S(1)}, f32[512]{0:T(512)}, u32[]{:S(2)}) copy-start(f32[512]{0:T(512)} %get-tuple-element.24) | copy-start | bytes 6148
  281.6 111.2 %copy-start.87 = (f32[1,512]{1,0:T(1,128)}, f32[1,512]{1,0:T(1,128)S(1)}, u32[]{:S(2)}) copy-start(f32[1,512]{1,0:T(1,128)S(1)} %get-tuple-element.100) | copy-start | bytes 6148
  284.2 11.0 all-to-all-start
  360.4 32.5 %copy-start.84 = (f32[512]{0:T(512)}, f32[512]{0:T(512)S(1)}, u32[]{:S(2)}) copy-start(f32[512]{0:T(512)S(1)} %broadcast_multiply_fusion.8) | copy-start | bytes 6148
  361.5 31.4 %copy-start.89 = (f32[512]{0:T(512)}, f32[512]{0:T(512)S(1)}, u32[]{:S(2)}) copy-start(f32[512]{0:T(512)S(1)} %add_rsqrt_fusion) | copy-start | bytes 6148
  410.5 23.8 copy-start.51
  629.7 233.0 %all-to-all-start.3 = ((bf16[4,4,1152]{2,0,1:T(4,128)(2,1)}), bf16[4,4,1152]{2,0,1:T(4,128)(2,1)S(1)}, u32[]{:S(2)}, u32[]{:S(2)}) async-start(bf16[4,4,1152]{2,0,1:T(4,128)(2,1)} %bitcast.52), calls=%async_computation.3 | async-start | bytes 73728 | tf_op jit(solution)/shard_map/all_to_all | solution.py:223
  633.0 268.2 %all-reduce.27.cloned.1.call-start = ((), (), s32[]{:S(2)}) async-start(), calls=%async_computation.11 | async-start | bytes 188416 | tf_op jit(solution)/shard_map/psum | solution.py:255
  859.5 32.0 %copy-start.81 = (bf16[8,768]{1,0:T(8,128)(2,1)S(1)}, bf16[8,768]{1,0:T(8,128)(2,1)}, u32[]{:S(2)}) copy-start(bf16[8,768]{1,0:T(8,128)(2,1)} %copy-done.80) | copy-start | bytes 36868
  859.5 32.0 %copy-start.83 = (bf16[8,768]{1,0:T(8,128)(2,1)S(1)}, bf16[8,768]{1,0:T(8,128)(2,1)}, u32[]{:S(2)}) copy-start(bf16[8,768]{1,0:T(8,128)(2,1)} %copy-done.82) | copy-start | bytes 36868
  859.5 32.0 %copy-start.114 = (s32[8]{0:T(128)S(1)}, s32[8]{0:T(128)}, u32[]{:S(2)}) copy-start(s32[8]{0:T(128)} %eq.102) | copy-start | bytes 100
  862.6 10.8 all-to-all-start.2
  867.7 1177.6 %all-reduce.29.cloned.1.call-start = ((), (), s32[]{:S(2)}) async-start(), calls=%async_computation.12 | async-start | bytes 68911104 | tf_op jit(solution)/shard_map/psum | solution.py:255
  867.7 27.0 %copy-start.113 = (s32[8]{0:T(128)S(1)}, s32[8]{0:T(128)}, u32[]{:S(2)}) copy-start(s32[8]{0:T(128)} %eq.106) | copy-start | bytes 100
  897.9 1203.2 %all-reduce.23.cloned.1.call-start = ((), (), s32[]{:S(2)}) async-start(), calls=%async_computation.9 | async-start | bytes 188416 | tf_op jit(solution)/shard_map/psum | solution.py:255
  901.2 1264.3 %all-reduce.21.cloned.1.call-start = ((), (), s32[]{:S(2)}) async-start(), calls=%async_computation.8 | async-start | bytes 3538944 | tf_op jit(solution)/shard_map/psum | solution.py:265
  905.1 1678.6 %all-reduce.25.cloned.1.call-start = ((), (), s32[]{:S(2)}) async-start(), calls=%async_computation.10 | async-start | bytes 68911104 | tf_op jit(solution)/shard_map/psum | solution.py:255
  (125 other events, 836.3 us)
Sparse Core Ops, SparseCore 0:
  9.7 75.3 all-gather.9
  86.7 29.2 all-gather.11
  117.5 88.5 all-gather.13
  207.5 90.2 all-gather.15
  862.8 35.9 all-reduce.26
  902.8 1142.4 all-reduce.28
  2049.4 51.6 all-reduce.22
  2105.0 60.4 all-reduce.20
  2171.0 412.6 all-reduce.24
